TPU v7x, 32 devices: a whole 2x2x4 slice. The times are simulated.
32 devices in a mesh: patch: 8 (over y, x, core), mlp: 4 (over z).
Axes of the slice: x: 2, y: 2, z: 4, core: 2. Of those that a mesh axis runs over, the one named last changes fastest.
Arguments:
- latent: bfloat16 [2048, 2432], P('patch', 'mlp'), may hold values from -24 to 24
- split_list: int32 [8, 4], P('patch'), may hold values from 0 to 256, as said below
- modulation: float32 [1, 6, 2432], replicated, may hold values from -3 to 3
- w_qkv: bfloat16 [2432, 3, 1536], P(None, None, 'mlp'), may hold values from -0.125 to 0.125
- w_out: bfloat16 [1536, 2432], P('mlp'), may hold values from -0.15625 to 0.15625
- w_up: bfloat16 [2432, 5120], P(None, 'mlp'), may hold values from -0.125 to 0.125
- w_down: bfloat16 [5120, 2432], P('mlp'), may hold values from -0.078125 to 0.078125
- qk_gains: float32 [3, 64], replicated, may hold values from 1.6 to 2.4
- text_kv: bfloat16 [2, 1, 154, 1536], P(None, None, None, 'mlp'), may hold values from -6 to 6
- timestep: int32 [1], replicated, may hold values from 0 to 27
- step_sizes: float32 [28], replicated, may hold values from -0.6 to -0.1
Outputs:
- latent_next: bfloat16 [2048, 2432], P('patch', 'mlp')
Inputs may be any that keep to these rules, and one draw needn't show every extreme that they name: `split_list`: row d holds device d's tile pieces (item, count, item, count); over all devices the counts of every item add up to 1024. A device's two counts add up to at most 256, to exactly 256 on some device and to 0 on another. The devices holding an item's tokens form a run of consecutive indices of patch, taken cyclically. Both pieces may name the same item; they are then two parts of it.
All inputs are finite; a program needn't handle non-finite values.
Results may differ from a plain program's by a relative error of at most 0.0049.
Values may be sent and summed in bfloat16 or wider, within the bound.
A program may use at most 128 MiB of HBM per device.

v0:
```python
import jax
import jax.numpy as jnp
from jax import lax
from jax.sharding import PartitionSpec as P

HEAD = 64
norm_eps = 1e-06
block_rows = 512


def layer_norm(row_data):
    row_mean = jnp.mean(row_data, axis=-1, keepdims=True)
    centred = row_data - row_mean
    variance = jnp.mean(centred * centred, axis=-1, keepdims=True)
    return centred * lax.rsqrt(variance + norm_eps)


def head_norm(row_data, gain_row):
    shaped = row_data.reshape(row_data.shape[0], -1, HEAD)
    mean_square = jnp.mean(shaped * shaped, axis=-1, keepdims=True)
    return (shaped * lax.rsqrt(mean_square + norm_eps) * gain_row).reshape(row_data.shape)


def attend_dense(state_pair, queries, query_tags, key_rows, value_rows, key_tags):
    numerator, denominator = state_pair
    query_count = queries.shape[0]
    heads_here = queries.shape[1] // HEAD
    query_heads = queries.reshape(query_count, heads_here, HEAD)
    key_heads = key_rows.reshape(key_rows.shape[0], heads_here, HEAD)
    value_heads = value_rows.reshape(value_rows.shape[0], heads_here, HEAD)
    scores = jnp.einsum(
        "qhd,khd->qhk", query_heads, key_heads, preferred_element_type=jnp.float32
    ) * HEAD ** (-0.5)
    same_item = (query_tags[:, None] == key_tags[None, :])[:, None, :]
    weights = jnp.where(same_item, jnp.exp(scores), 0.0)
    denominator = denominator + jnp.sum(weights, axis=-1)
    numerator = numerator + jnp.einsum(
        "qhk,khd->qhd",
        weights.astype(jnp.bfloat16),
        value_heads,
        preferred_element_type=jnp.float32,
    )
    return (numerator, denominator)


def attend_block(state_pair, queries, query_tags, key_rows, value_rows, key_tags):
    touching = jnp.any(query_tags[:, None] == key_tags[None, :])

    def work(inner):
        return attend_dense(inner, queries, query_tags, key_rows, value_rows, key_tags)

    def skip(inner):
        return inner

    return lax.cond(touching, work, skip, state_pair)


def attend(state_pair, queries, query_tags, key_rows, value_rows, key_tags):
    key_count = key_rows.shape[0]
    if key_count > 2 * block_rows and key_count % block_rows == 0:

        def one_block(block_index, inner):
            offset = block_index * block_rows
            return attend_block(
                inner,
                queries,
                query_tags,
                lax.dynamic_slice_in_dim(key_rows, offset, block_rows, 0),
                lax.dynamic_slice_in_dim(value_rows, offset, block_rows, 0),
                lax.dynamic_slice_in_dim(key_tags, offset, block_rows, 0),
            )

        return lax.fori_loop(0, key_count // block_rows, one_block, state_pair)
    return attend_block(state_pair, queries, query_tags, key_rows, value_rows, key_tags)


def body(
    latent,
    split_list,
    modulation,
    w_qkv,
    w_out,
    w_up,
    w_down,
    qk_gains,
    text_kv,
    timestep,
    step_sizes,
):
    share_cols = latent.shape[1]
    row_data = lax.all_gather(latent, "mlp", axis=1, tiled=True)
    capacity = row_data.shape[0]
    item_total = modulation.shape[0]
    item_a = split_list[0, 0]
    count_a = split_list[0, 1]
    item_b = split_list[0, 2]
    count_b = split_list[0, 3]
    slot_ids = jnp.arange(capacity, dtype=jnp.int32)
    in_first = slot_ids < count_a
    slot_live = slot_ids < count_a + count_b
    slot_item = jnp.where(in_first, item_a, jnp.where(slot_live, item_b, -1))
    item_ids = jnp.arange(item_total, dtype=jnp.int32)
    one_hot = (slot_item[:, None] == item_ids[None, :]).astype(jnp.float32)
    slot_mods = jnp.dot(
        one_hot,
        modulation.reshape(item_total, -1),
        precision=lax.Precision.HIGHEST,
        preferred_element_type=jnp.float32,
    ).reshape(capacity, 6, -1)
    slot_step = jnp.dot(
        one_hot,
        jnp.take(step_sizes, timestep),
        precision=lax.Precision.HIGHEST,
        preferred_element_type=jnp.float32,
    )
    float_rows = row_data.astype(jnp.float32)
    normed_one = (layer_norm(float_rows) * (1.0 + slot_mods[:, 1]) + slot_mods[:, 0]).astype(
        jnp.bfloat16
    )
    projected = jnp.einsum("nd,dch->nch", normed_one, w_qkv, preferred_element_type=jnp.float32)
    queries = head_norm(projected[:, 0], qk_gains[0]).astype(jnp.bfloat16)
    key_rows = head_norm(projected[:, 1], qk_gains[1]).astype(jnp.bfloat16)
    value_rows = projected[:, 2].astype(jnp.bfloat16)
    head_cols = queries.shape[1]
    heads_here = head_cols // HEAD
    text_pair = jnp.take(text_kv, jnp.stack([item_a, item_b]), axis=1)
    text_keys = head_norm(
        text_pair[0].reshape(-1, head_cols).astype(jnp.float32), qk_gains[2]
    ).astype(jnp.bfloat16)
    text_values = text_pair[1].reshape(-1, head_cols)
    second_tag = jnp.where(item_b != item_a, item_b, -2)
    text_tags = jnp.repeat(jnp.stack([item_a, second_tag]), text_kv.shape[2]).astype(jnp.bfloat16)
    query_tags = slot_item.astype(jnp.bfloat16)
    key_tags = jnp.where(slot_live, slot_item, -3).astype(jnp.bfloat16)
    empty_state = (
        jnp.zeros((capacity, heads_here, HEAD), jnp.float32),
        jnp.zeros((capacity, heads_here), jnp.float32),
    )
    start_state = attend(empty_state, queries, query_tags, text_keys, text_values, text_tags)
    numerator, denominator = attend(
        start_state,
        queries,
        query_tags,
        lax.all_gather(key_rows, "patch", axis=0, tiled=True),
        lax.all_gather(value_rows, "patch", axis=0, tiled=True),
        lax.all_gather(key_tags, "patch", axis=0, tiled=True),
    )
    safe_denominator = denominator + (slot_item < 0).astype(jnp.float32)[:, None]
    attended = (
        (numerator / safe_denominator[:, :, None]).reshape(capacity, head_cols).astype(jnp.bfloat16)
    )
    head_part = jnp.dot(attended, w_out, preferred_element_type=jnp.float32)
    col_first = lax.axis_index("mlp") * share_cols
    attn_total = lax.psum(head_part, "mlp")
    after_attn = float_rows + slot_mods[:, 2] * attn_total
    normed_two = (layer_norm(after_attn) * (1.0 + slot_mods[:, 4]) + slot_mods[:, 3]).astype(
        jnp.bfloat16
    )
    up_total = jnp.dot(normed_two, w_up, preferred_element_type=jnp.float32)
    attn_share = lax.dynamic_slice_in_dim(after_attn, col_first, share_cols, 1)
    hidden_units = jax.nn.gelu(up_total, approximate=True).astype(jnp.bfloat16)
    unit_part = jnp.dot(hidden_units, w_down, preferred_element_type=jnp.float32)
    unit_total = lax.psum_scatter(unit_part, "mlp", scatter_dimension=1, tiled=True)
    gate_share = lax.dynamic_slice_in_dim(slot_mods[:, 5], col_first, share_cols, 1)
    after_mlp = attn_share + gate_share * unit_total
    next_rows = latent.astype(jnp.float32) + slot_step[:, None] * after_mlp
    return jnp.where(slot_live[:, None], next_rows, 0.0).astype(jnp.bfloat16)


def solution(mesh):
    return jax.shard_map(
        body,
        mesh=mesh,
        in_specs=(
            P("patch", "mlp"),
            P("patch", None),
            P(),
            P(None, None, "mlp"),
            P("mlp", None),
            P(None, "mlp"),
            P("mlp", None),
            P(),
            P(None, None, None, "mlp"),
            P(),
            P(),
        ),
        out_specs=P("patch", "mlp"),
        check_vma=False,
    )
```

profile of v0, /device:TPU:0, one launch (start us, length us, event | category | flops | bytes accessed | tf_op | source)
XLA Modules:
  0.0 319.1 jit_solution(8434744912893777445)
XLA Ops:
  15.4 6.1 %broadcast_multiply_fusion = f32[256,6,2432]{0,2,1:T(8,128)} fusion(f32[6,2432]{1,0:T(8,128)S(1)} %bitcast.153, f32[256]{0:T(256)S(1)} %get-tuple-element.424), kind=kLoop, calls=%fused_computation.23 | loop fusion | flops 3735552 | bytes 15001600 | tf_op jit(solution)/shard_map/dot_general | solution.py:104
  21.6 21.7 %all-gather.6.cloned.1.call-done = bf16[256,2432]{0,1:T(8,128)(2,1)} async-done(((bf16[256,608]{0,1:T(8,128)(2,1)}), bf16[256,2432]{0,1:T(8,128)(2,1)}) %all-gather.6.cloned.1.call-update) | async-done | bytes 1245200 | tf_op jit(solution)/shard_map/all_gather | solution.py:91
  46.7 6.0 %fusion.44 = f32[256,3,384]{2,0,1:T(8,128)S(1)} fusion(bf16[2432,3,384]{2,0,1:T(8,128)(2,1)} %param.20, f32[256,6,2432]{0,2,1:T(8,128)} %broadcast_multiply_fusion, bf16[256,2432]{0,1:T(8,128)(2,1)S(1)} %copy-done.2, f32[256]{0:T(256)S(1)} %add_rsqrt_fusion.4, f32[256]{0:T(256)S(1)} %broadcast_multiply_fusion.2), kind=kOutput, calls=%fused_computation.58 | convolution fusion | flops 1438810112 | bytes 13010944 | tf_op jit(solution)/shard_map/nd,dch->nch/dot_general | solution.py:120
  61.2 2.1 fusion.60
  75.1 2.6 reshape.303
  79.7 2.2 fusion.63
  81.9 2.6 mul.193
  86.5 2.1 copy.95
  88.7 9.0 %all-gather.1 = bf16[8,1,256]{2,1,0:T(2,128)(2,1)S(1)} all-gather(bf16[1,1,256]{2,1,0:T(2,128)(2,1)S(1)} %reshape.300), channel_id=1, replica_groups=mesh['patch'=8,'mlp'=4] {'patch'}, dimensions={0}, use_global_device_ids=true | all-gather | bytes 4608 | tf_op jit(solution)/shard_map/all_gather | solution.py:146
  100.5 8.4 %conditional.2 = (f32[256,6,64]{0,2,1:T(8,128)S(1)}, f32[256,6]{0,1:T(8,128)S(1)}) conditional(s32[]{:T(128)} %convert_element_type.111, () %tuple.38, (bf16[256]{0:T(256)(128)(2,1)S(1)}, s32[2]{0:T(128)S(1)}, bf16[308,384]{1,0:T(8,128)(2,1)}, bf16[256,384]{1,0:T(8,128)(2,1)S(1)}, bf16[2,2,154,384]{2,1,3,0:T(2,128)(2,1)}) %tuple.110), branch_computations={%region_5.6_spmd, %region_6.8_spmd} | conditional | flops 123080192 | bytes 5880796 | solution.py:55
  108.9 2.6 copy.105
  111.5 2.6 copy.103
  114.1 29.6 %while.17 = (s32[]{:T(128)}, f32[256,6,64]{0,2,1:T(8,128)S(1)}, f32[256,6]{0,1:T(8,128)S(1)}, bf16[2048]{0:T(1024)(128)(2,1)S(1)}, bf16[2048,384]{0,1:T(8,128)(2...) while((s32[]{:T(128)}, f32[256,6,64]{0,2,1:T(8,128)S(1)}, ...), condition=%wide.region_14.15_spmd.clone, body=%wide.region_9.14_spmd.clone.sunk | while | flops 206537984 | bytes 10057545 | solution.py:73
  117.6 3.9 %conditional.5 = ((f32[256,6,64]{0,2,1:T(8,128)S(1)}, f32[256,6]{0,1:T(8,128)S(1)})) conditional(s32[]{:T(128)} %convert_element_type.190, (f32[256,6,64]{0,2,1:T(8,128)S(1)}, f32[256,6]{0,1:T(8,128)S(1)}) %tuple.89, (bf16[256]{0:T(256)(128)(2,1)S(1)}, bf16[512]{0:T(512)(128)(2,1)S(1)}, bf16[2048,384]{0,1:T(8,128)(2,1)}, s32[]{:T(128)}, ...), branch_computations={%region_11.11_spmd, %region_12.13_spmd} | conditional | flops 206274560 | bytes 10053148 | solution.py:55
  125.0 3.9 %conditional.5 = ((f32[256,6,64]{0,2,1:T(8,128)S(1)}, f32[256,6]{0,1:T(8,128)S(1)})) conditional(s32[]{:T(128)} %convert_element_type.190, (f32[256,6,64]{0,2,1:T(8,128)S(1)}, f32[256,6]{0,1:T(8,128)S(1)}) %tuple.89, (bf16[256]{0:T(256)(128)(2,1)S(1)}, bf16[512]{0:T(512)(128)(2,1)S(1)}, bf16[2048,384]{0,1:T(8,128)(2,1)}, s32[]{:T(128)}, ...), branch_computations={%region_11.11_spmd, %region_12.13_spmd} | conditional | flops 206274560 | bytes 10053148 | solution.py:55
  132.4 3.9 %conditional.5 = ((f32[256,6,64]{0,2,1:T(8,128)S(1)}, f32[256,6]{0,1:T(8,128)S(1)})) conditional(s32[]{:T(128)} %convert_element_type.190, (f32[256,6,64]{0,2,1:T(8,128)S(1)}, f32[256,6]{0,1:T(8,128)S(1)}) %tuple.89, (bf16[256]{0:T(256)(128)(2,1)S(1)}, bf16[512]{0:T(512)(128)(2,1)S(1)}, bf16[2048,384]{0,1:T(8,128)(2,1)}, s32[]{:T(128)}, ...), branch_computations={%region_11.11_spmd, %region_12.13_spmd} | conditional | flops 206274560 | bytes 10053148 | solution.py:55
  139.8 3.9 %conditional.5 = ((f32[256,6,64]{0,2,1:T(8,128)S(1)}, f32[256,6]{0,1:T(8,128)S(1)})) conditional(s32[]{:T(128)} %convert_element_type.190, (f32[256,6,64]{0,2,1:T(8,128)S(1)}, f32[256,6]{0,1:T(8,128)S(1)}) %tuple.89, (bf16[256]{0:T(256)(128)(2,1)S(1)}, bf16[512]{0:T(512)(128)(2,1)S(1)}, bf16[2048,384]{0,1:T(8,128)(2,1)}, s32[]{:T(128)}, ...), branch_computations={%region_11.11_spmd, %region_12.13_spmd} | conditional | flops 206274560 | bytes 10053148 | solution.py:55
  143.8 2.4 fusion.75
  146.3 98.0 %all-reduce.2.cloned.1.call-done = f32[256,2432]{0,1:T(8,128)} async-done(((f32[256,2432]{0,1:T(8,128)}), f32[256,2432]{0,1:T(8,128)}) %all-reduce.2.cloned.1.call-update) | async-done | bytes 2490384 | tf_op jit(solution)/shard_map/psum | solution.py:154
  244.3 2.9 fusion.71
  249.0 12.0 %convolution_bitcast_fusion.1 = f32[2432,256]{1,0:T(8,128)} fusion(bf16[1280,2432]{1,0:T(8,128)(2,1)} %param.23, bf16[2432,1280]{1,0:T(8,128)(2,1)} %param.22, f32[256,6,2432]{0,2,1:T(8,128)} %broadcast_multiply_fusion, f32[256,2432]{0,1:T(8,128)} %copy-done.1, f32[256]{0:T(256)S(1)} %add_rsqrt_fusion.3, f32[256]{0:T(256)S(1)} %broadcast_multiply_fusion.1), kind=kOutput, calls=%fused_computation.24 | convolution fusion | flops 3194355712 | bytes 22415360
  261.0 3.4 %slice.85 = f32[256,1,2432]{0,2,1:T(8,128)} slice(f32[256,6,2432]{0,2,1:T(8,128)} %broadcast_multiply_fusion), slice={[0:256], [5:6], [0:2432]} | slice | bytes 4980736 | tf_op jit(solution)/shard_map/slice | solution.py:164
  264.4 45.9 %reduce-scatter.4.cloned.1.call-done = f32[608,256]{1,0:T(8,128)} async-done(((f32[2432,256]{1,0:T(8,128)}), f32[608,256]{1,0:T(8,128)}) %reduce-scatter.4.cloned.1.call-update) | async-done | bytes 622608
  310.3 2.3 fusion.58
  (122 shorter events, 70.9 us)
Async XLA Ops:
  6.5 137.3 %copy-start = (bf16[384,2432]{1,0:T(8,128)(2,1)S(1)}, bf16[384,2432]{1,0:T(8,128)(2,1)}, u32[]{:S(2)}) copy-start(bf16[384,2432]{1,0:T(8,128)(2,1)} %param.21) | copy-start | bytes 5603332
  6.5 36.7 %all-gather.6.cloned.1.call-start = ((), (), s32[]{:S(2)}) async-start(), calls=%async_computation.1 | async-start | bytes 1556480 | tf_op jit(solution)/shard_map/all_gather | solution.py:91
  7.3 101.7 %all-gather.10.cloned.1.call-start = ((), (), s32[]{:S(2)}) async-start(), calls=%async_computation.4 | async-start | bytes 1769472 | tf_op jit(solution)/shard_map/all_gather | solution.py:145
  43.2 3.4 %copy-start.2 = (bf16[256,2432]{0,1:T(8,128)(2,1)S(1)}, bf16[256,2432]{0,1:T(8,128)(2,1)}, u32[]{:S(2)}) copy-start(bf16[256,2432]{0,1:T(8,128)(2,1)} %all-gather.6.cloned.1.call-done) | copy-start | bytes 3735556
  46.7 7.9 %copy-start.7 = (f32[3,64]{1,0:T(4,128)S(1)}, f32[3,64]{1,0:T(4,128)}, u32[]{:S(2)}) copy-start(f32[3,64]{1,0:T(4,128)} %param.24) | copy-start | bytes 2308
  52.7 1.0 copy-start.4
  54.5 57.1 %all-gather.8.cloned.1.call-start = ((), (), s32[]{:S(2)}) async-start(), calls=%async_computation.2 | async-start | bytes 1769472 | tf_op jit(solution)/shard_map/all_gather | solution.py:144
  63.3 181.0 %all-reduce.2.cloned.1.call-start = ((), (), s32[]{:S(2)}) async-start(), calls=%async_computation.3 | async-start | bytes 4980736 | tf_op jit(solution)/shard_map/psum | solution.py:154
  72.9 0.9 copy-start.3
  106.6 1.7 copy-start.6
  146.3 164.0 %reduce-scatter.4.cloned.1.call-start = ((), (), s32[]{:S(2)}) async-start(), calls=%async_computation.5 | async-start | bytes 3112960
  247.2 1.4 copy-start.1
  261.0 49.3 %copy-start.5 = (bf16[256,608]{0,1:T(8,128)(2,1)S(1)}, bf16[256,608]{0,1:T(8,128)(2,1)}, u32[]{:S(2)}) copy-start(bf16[256,608]{0,1:T(8,128)(2,1)} %param.17) | copy-start | bytes 933892
Sparse Core Ops, SparseCore 0:
  8.9 34.2 all-gather.5
  54.6 24.7 all-gather.9
  81.3 25.7 all-gather.7
  146.4 97.8 all-reduce.1
  261.1 49.0 reduce-scatter.3
where the time goes:
time: 321 us; the launch traced here: 319 us
  waiting for transfers between devices  166 us (52%)
  local copies, waits for them, and re-layouts  45.1 us (14%)
  other arithmetic  44.3 us (14%)
  matrix products  32.5 us (10%)
  between operations  18.6 us (6%)
  blocking collectives  9.01 us (3%)
    psum x1, waiting for transfers between devices, body(): attn_total = lax.psum(head_part, 'mlp')  98 us
    unnamed x6, waiting for transfers between devices  46.6 us
    all_gather x1, waiting for transfers between devices, body(): row_data = lax.all_gather(latent, 'mlp', axis=1, tiled=True)  21.7 us
    unnamed x1, matrix products  12 us
    unnamed x20, local copies, waits for them, and re-layouts  10.3 us
    all_gather x1, blocking collectives, body(): lax.all_gather(key_tags, 'patch', axis=0, tiled=True)  9.01 us
    dot_general x5, matrix products, attend_dense(): jnp.einsum('qhd,khd->qhk', query_heads, key_heads, preferred_element_type...  8.96 us
    convert_element_type x4, other arithmetic, body(): query_tags = slot_item.astype(jnp.bfloat16)  7.74 us
  transfers between devices with their start and end apart: 5, of which 3 were waited for; matrix products, arithmetic and copies ran while one was open for 18% of the time, Pallas kernels for 0%

commit v1 on v0

--- a/solution.py
+++ b/solution.py
@@ -151,7 +151,11 @@
     )
     head_part = jnp.dot(attended, w_out, preferred_element_type=jnp.float32)
     col_first = lax.axis_index("mlp") * share_cols
-    attn_total = lax.psum(head_part, "mlp")
+    attn_total = head_part
+    for hop in (1, 2):
+        attn_total = attn_total + lax.ppermute(
+            attn_total, "mlp", [(dev, dev ^ hop) for dev in range(4)]
+        )
     after_attn = float_rows + slot_mods[:, 2] * attn_total
     normed_two = (layer_norm(after_attn) * (1.0 + slot_mods[:, 4]) + slot_mods[:, 3]).astype(
         jnp.bfloat16

time: 321 us -> 386 us (1.20)
  waiting for transfers between devices: 166 us -> 231 us
    ppermute x0 -> x2, waiting for transfers between devices: none -> 164 us  [body(): lax.ppermute(attn_total, 'mlp', [(dev, dev ^ hop) for dev in range(4)])]
    psum x1 -> x0, waiting for transfers between devices: 98 us -> none  [body(): attn_total = lax.psum(head_part, 'mlp')]
    unnamed x6 -> x5, waiting for transfers between devices: 46.6 us -> 45.7 us
  transfers between devices with their start and end apart: 5 -> 6, of which waited for: 3 -> 4; matrix products, arithmetic and copies ran while one was open for 18% -> 15% of each run, Pallas kernels for 0% -> 0%
where the time goes in v1:
time: 386 us; the launch traced here: 384 us
  waiting for transfers between devices  231 us (60%)
  local copies, waits for them, and re-layouts  45.1 us (12%)
  other arithmetic  44.2 us (11%)
  matrix products  31.1 us (8%)
  between operations  18.5 us (5%)
  blocking collectives  8.8 us (2%)
    ppermute x2, waiting for transfers between devices, body(): lax.ppermute(attn_total, 'mlp', [(dev, dev ^ hop) for dev in range(4)])  164 us
    unnamed x5, waiting for transfers between devices  45.7 us
    all_gather x1, waiting for transfers between devices, body(): row_data = lax.all_gather(latent, 'mlp', axis=1, tiled=True)  21.6 us
    unnamed x1, matrix products  12 us
    unnamed x20, local copies, waits for them, and re-layouts  10.3 us
    dot_general x5, matrix products, attend_dense(): jnp.einsum('qhd,khd->qhk', query_heads, key_heads, preferred_element_type...  8.96 us
    all_gather x1, blocking collectives, body(): lax.all_gather(key_tags, 'patch', axis=0, tiled=True)  8.8 us
  transfers between devices with their start and end apart: 6, of which 4 were waited for; matrix products, arithmetic and copies ran while one was open for 15% of the time, Pallas kernels for 0%

profile of v1, /device:TPU:0, one launch (start us, length us, event | category | flops | bytes accessed | tf_op | source)
XLA Modules:
  0.0 384.3 jit_solution(3827176584083084665)
XLA Ops:
  15.5 6.1 %broadcast_multiply_fusion = f32[256,6,2432]{0,2,1:T(8,128)} fusion(f32[6,2432]{1,0:T(8,128)S(1)} %bitcast.153, f32[256]{0:T(256)S(1)} %get-tuple-element.424), kind=kLoop, calls=%fused_computation.23 | loop fusion | flops 3735552 | bytes 15001600 | tf_op jit(solution)/shard_map/dot_general | solution.py:104
  21.6 21.6 %all-gather.6.cloned.1.call-done = bf16[256,2432]{0,1:T(8,128)(2,1)} async-done(((bf16[256,608]{0,1:T(8,128)(2,1)}), bf16[256,2432]{0,1:T(8,128)(2,1)}) %all-gather.6.cloned.1.call-update) | async-done | bytes 1245200 | tf_op jit(solution)/shard_map/all_gather | solution.py:91
  46.7 6.0 %fusion.44 = f32[256,3,384]{2,0,1:T(8,128)S(1)} fusion(bf16[2432,3,384]{2,0,1:T(8,128)(2,1)} %param.20, f32[256,6,2432]{0,2,1:T(8,128)} %broadcast_multiply_fusion, bf16[256,2432]{0,1:T(8,128)(2,1)S(1)} %copy-done.2, f32[256]{0:T(256)S(1)} %add_rsqrt_fusion.4, f32[256]{0:T(256)S(1)} %broadcast_multiply_fusion.2), kind=kOutput, calls=%fused_computation.58 | convolution fusion | flops 1438810112 | bytes 13010944 | tf_op jit(solution)/shard_map/nd,dch->nch/dot_general | solution.py:120
  61.2 2.1 fusion.60
  74.8 2.6 reshape.303
  79.5 2.2 fusion.63
  81.7 2.6 mul.193
  86.3 2.1 copy.95
  88.5 8.8 %all-gather.1 = bf16[8,1,256]{2,1,0:T(2,128)(2,1)S(1)} all-gather(bf16[1,1,256]{2,1,0:T(2,128)(2,1)S(1)} %reshape.300), channel_id=1, replica_groups=mesh['patch'=8,'mlp'=4] {'patch'}, dimensions={0}, use_global_device_ids=true | all-gather | bytes 4608 | tf_op jit(solution)/shard_map/all_gather | solution.py:146
  100.1 8.4 %conditional.2 = (f32[256,6,64]{0,2,1:T(8,128)S(1)}, f32[256,6]{0,1:T(8,128)S(1)}) conditional(s32[]{:T(128)} %convert_element_type.111, () %tuple.38, (bf16[256]{0:T(256)(128)(2,1)S(1)}, s32[2]{0:T(128)S(1)}, bf16[308,384]{1,0:T(8,128)(2,1)}, bf16[256,384]{1,0:T(8,128)(2,1)S(1)}, bf16[2,2,154,384]{2,1,3,0:T(2,128)(2,1)}) %tuple.108), branch_computations={%region_5.6_spmd, %region_6.8_spmd} | conditional | flops 123080192 | bytes 5880796 | solution.py:55
  108.5 2.6 copy.105
  111.1 2.6 copy.103
  113.7 29.6 %while.17 = (s32[]{:T(128)}, f32[256,6,64]{0,2,1:T(8,128)S(1)}, f32[256,6]{0,1:T(8,128)S(1)}, bf16[2048]{0:T(1024)(128)(2,1)S(1)}, bf16[2048,384]{0,1:T(8,128)(2...) while((s32[]{:T(128)}, f32[256,6,64]{0,2,1:T(8,128)S(1)}, ...), condition=%wide.region_14.15_spmd.clone, body=%wide.region_9.14_spmd.clone.sunk | while | flops 206537984 | bytes 10057545 | solution.py:73
  117.2 3.9 %conditional.5 = ((f32[256,6,64]{0,2,1:T(8,128)S(1)}, f32[256,6]{0,1:T(8,128)S(1)})) conditional(s32[]{:T(128)} %convert_element_type.190, (f32[256,6,64]{0,2,1:T(8,128)S(1)}, f32[256,6]{0,1:T(8,128)S(1)}) %tuple.89, (bf16[256]{0:T(256)(128)(2,1)S(1)}, bf16[512]{0:T(512)(128)(2,1)S(1)}, bf16[2048,384]{0,1:T(8,128)(2,1)}, s32[]{:T(128)}, ...), branch_computations={%region_11.11_spmd, %region_12.13_spmd} | conditional | flops 206274560 | bytes 10053148 | solution.py:55
  124.6 3.9 %conditional.5 = ((f32[256,6,64]{0,2,1:T(8,128)S(1)}, f32[256,6]{0,1:T(8,128)S(1)})) conditional(s32[]{:T(128)} %convert_element_type.190, (f32[256,6,64]{0,2,1:T(8,128)S(1)}, f32[256,6]{0,1:T(8,128)S(1)}) %tuple.89, (bf16[256]{0:T(256)(128)(2,1)S(1)}, bf16[512]{0:T(512)(128)(2,1)S(1)}, bf16[2048,384]{0,1:T(8,128)(2,1)}, s32[]{:T(128)}, ...), branch_computations={%region_11.11_spmd, %region_12.13_spmd} | conditional | flops 206274560 | bytes 10053148 | solution.py:55
  132.0 3.9 %conditional.5 = ((f32[256,6,64]{0,2,1:T(8,128)S(1)}, f32[256,6]{0,1:T(8,128)S(1)})) conditional(s32[]{:T(128)} %convert_element_type.190, (f32[256,6,64]{0,2,1:T(8,128)S(1)}, f32[256,6]{0,1:T(8,128)S(1)}) %tuple.89, (bf16[256]{0:T(256)(128)(2,1)S(1)}, bf16[512]{0:T(512)(128)(2,1)S(1)}, bf16[2048,384]{0,1:T(8,128)(2,1)}, s32[]{:T(128)}, ...), branch_computations={%region_11.11_spmd, %region_12.13_spmd} | conditional | flops 206274560 | bytes 10053148 | solution.py:55
  139.4 3.9 %conditional.5 = ((f32[256,6,64]{0,2,1:T(8,128)S(1)}, f32[256,6]{0,1:T(8,128)S(1)})) conditional(s32[]{:T(128)} %convert_element_type.190, (f32[256,6,64]{0,2,1:T(8,128)S(1)}, f32[256,6]{0,1:T(8,128)S(1)}) %tuple.89, (bf16[256]{0:T(256)(128)(2,1)S(1)}, bf16[512]{0:T(512)(128)(2,1)S(1)}, bf16[2048,384]{0,1:T(8,128)(2,1)}, s32[]{:T(128)}, ...), branch_computations={%region_11.11_spmd, %region_12.13_spmd} | conditional | flops 206274560 | bytes 10053148 | solution.py:55
  145.2 55.5 %collective-permute-done = f32[256,2432]{0,1:T(8,128)S(1)} collective-permute-done((f32[256,2432]{0,1:T(8,128)S(1)}, f32[256,2432]{0,1:T(8,128)S(1)}, u32[]{:S(2)}, u32[]{:S(2)}) %collective-permute-start) | collective-permute-done | bytes 2490400 | tf_op jit(solution)/shard_map/ppermute | solution.py:156
  202.5 108.3 %collective-permute-done.1 = f32[256,2432]{0,1:T(8,128)S(1)} collective-permute-done((f32[256,2432]{0,1:T(8,128)S(1)}, f32[256,2432]{0,1:T(8,128)S(1)}, u32[]{:S(2)}, u32[]{:S(2)}) %collective-permute-start.1) | collective-permute-done | bytes 2490400 | tf_op jit(solution)/shard_map/ppermute | solution.py:156
  310.8 2.4 fusion.71
  315.0 12.0 %convolution_bitcast_fusion.1 = f32[2432,256]{1,0:T(8,128)} fusion(bf16[1280,2432]{1,0:T(8,128)(2,1)} %param.23, bf16[2432,1280]{1,0:T(8,128)(2,1)} %param.22, f32[256,6,2432]{0,2,1:T(8,128)} %broadcast_multiply_fusion, f32[256,2432]{0,1:T(8,128)} %copy-done.1, f32[256]{0:T(256)S(1)} %add_rsqrt_fusion.3, f32[256]{0:T(256)S(1)} %broadcast_multiply_fusion.1), kind=kOutput, calls=%fused_computation.24 | convolution fusion | flops 3194355712 | bytes 22415360
  327.1 3.4 slice.85
  330.5 44.9 %reduce-scatter.4.cloned.1.call-done = f32[608,256]{1,0:T(8,128)} async-done(((f32[2432,256]{1,0:T(8,128)}), f32[608,256]{1,0:T(8,128)}) %reduce-scatter.4.cloned.1.call-update) | async-done | bytes 622608
  375.4 2.3 fusion.58
  (124 shorter events, 74.5 us)
Async XLA Ops:
  6.5 136.8 %copy-start = (bf16[384,2432]{1,0:T(8,128)(2,1)S(1)}, bf16[384,2432]{1,0:T(8,128)(2,1)}, u32[]{:S(2)}) copy-start(bf16[384,2432]{1,0:T(8,128)(2,1)} %param.21) | copy-start | bytes 5603332
  6.5 36.7 %all-gather.6.cloned.1.call-start = ((), (), s32[]{:S(2)}) async-start(), calls=%async_computation.1 | async-start | bytes 1556480 | tf_op jit(solution)/shard_map/all_gather | solution.py:91
  7.3 101.2 %all-gather.10.cloned.1.call-start = ((), (), s32[]{:S(2)}) async-start(), calls=%async_computation.3 | async-start | bytes 1769472 | tf_op jit(solution)/shard_map/all_gather | solution.py:145
  43.2 3.4 copy-start.2
  46.7 7.9 %copy-start.7 = (f32[3,64]{1,0:T(4,128)S(1)}, f32[3,64]{1,0:T(4,128)}, u32[]{:S(2)}) copy-start(f32[3,64]{1,0:T(4,128)} %param.24) | copy-start | bytes 2308
  52.7 1.0 copy-start.4
  54.5 56.6 %all-gather.8.cloned.1.call-start = ((), (), s32[]{:S(2)}) async-start(), calls=%async_computation.2 | async-start | bytes 1769472 | tf_op jit(solution)/shard_map/all_gather | solution.py:144
  63.3 312.1 %reduce-scatter.4.cloned.1.call-start = ((), (), s32[]{:S(2)}) async-start(), calls=%async_computation.4 | async-start | bytes 3112960
  72.7 0.9 copy-start.3
  106.2 1.8 copy-start.6
  144.3 56.3 %collective-permute-start = (f32[256,2432]{0,1:T(8,128)S(1)}, f32[256,2432]{0,1:T(8,128)S(1)}, u32[]{:S(2)}, u32[]{:S(2)}) collective-permute-start(f32[256,2432]{0,1:T(8,128)S(1)} %fusion.75), channel_id=1, source_target_pairs={{0,1},{1,0},{2,3},{3,2},{4,5},{5,4},{6,7},{7,6},{8,9},{9,8},{10,11... | collective-permute-start | bytes 7471112 | tf_op jit(solution)/shard_map/ppermute | solution.py:156
  201.0 109.8 %collective-permute-start.1 = (f32[256,2432]{0,1:T(8,128)S(1)}, f32[256,2432]{0,1:T(8,128)S(1)}, u32[]{:S(2)}, u32[]{:S(2)}) collective-permute-start(f32[256,2432]{0,1:T(8,128)S(1)} %add.170), channel_id=1, source_target_pairs={{0,2},{1,3},{2,0},{3,1},{4,6},{5,7},{6,4},{7,5},{8,10},{9,11},{10,... | collective-permute-start | bytes 7471112 | tf_op jit(solution)/shard_map/ppermute | solution.py:156
  313.2 1.4 copy-start.1
  327.1 48.3 %copy-start.5 = (bf16[256,608]{0,1:T(8,128)(2,1)S(1)}, bf16[256,608]{0,1:T(8,128)(2,1)}, u32[]{:S(2)}) copy-start(bf16[256,608]{0,1:T(8,128)(2,1)} %param.17) | copy-start | bytes 933892
Sparse Core Ops, SparseCore 0:
  8.9 34.2 all-gather.5
  54.6 24.7 all-gather.9
  81.3 25.6 all-gather.7
  327.2 48.1 reduce-scatter.3
